TPU v7x, 32 devices: a whole 2x2x4 slice. The times are simulated.
32 devices in a mesh: ctx: 8 (over y, x, core), db: 4 (over z).
Axes of the slice: x: 2, y: 2, z: 4, core: 2. Of those that a mesh axis runs over, the one named last changes fastest.
Arguments:
- stream: bfloat16 [3072, 4096], P('ctx', 'db'), may hold values from -6 to 6
- history: bfloat16 [8, 3072, 4096], P(None, 'ctx', 'db'), may hold values from -6 to 6
- dwa_weights: float32 [9], replicated, may hold values from -0.5 to 1
- w_query: bfloat16 [4096, 4096], P('ctx', 'db'), may hold values from -0.09375 to 0.09375
- w_out: bfloat16 [4096, 4096], P('db', 'ctx'), may hold values from -0.125 to 0.125
- encoded_kv: bfloat16 [4, 24, 128, 2, 4096], P('db', None, 'ctx'), may hold values from -340 to 340
- neighbour_ids: int32 [96], replicated, may hold values from 0 to 95, each once
Outputs:
- block_out: bfloat16 [3072, 4096], P('ctx', 'db')
- dense: bfloat16 [3072, 4096], P('ctx', 'db')
Inputs may be any that keep to these rules, and one draw needn't show every extreme that they name: `neighbour_ids`: each stored neighbour is named by exactly one slot.
All inputs are finite; a program needn't handle non-finite values.
Results may differ from a plain program's by a relative error of at most 0.014.
The roundings to bfloat16 on the way count: a program that leaves them out, or rounds other values in their place, can miss the bound.
Values may be sent and summed in bfloat16 or wider, within the bound.
A program may use at most 128 MiB of HBM per device.

v0:
```python
import functools

import jax
import jax.numpy as jnp
from jax import lax
from jax.experimental import pallas as pl
from jax.experimental.pallas import tpu as pltpu
from jax.sharding import PartitionSpec as P

HDIM = 128
SPAN = 64
NNB = 2
MESH = pl.DeviceIdType.MESH


def shifted(block, axis, distance):
    devices = range(lax.axis_size(axis))
    route = [(i - distance, i) for i in devices if i - distance in devices]
    return lax.ppermute(block, axis, route)


def exchange_kernel(n_ctx, n_db, chunks, ids, kv, out, *scratch):
    stores, outgoing = scratch[:chunks], scratch[chunks : 2 * chunks]
    z_send, z_recv, z_local, c_send, c_recv, c_local = scratch[2 * chunks :]
    c, d = lax.axis_index("ctx"), lax.axis_index("db")
    group_size = kv.shape[1]
    width = stores[0].shape[3]
    heads = width // HDIM
    requests = out.shape[1]
    barrier = pltpu.get_barrier_semaphore()
    for r in range(1, n_db):
        pl.semaphore_signal(barrier, inc=1, device_id=(c, lax.rem(d + r, n_db)), device_id_type=MESH)
    for r in range(1, n_ctx):
        pl.semaphore_signal(barrier, inc=1, device_id=(lax.rem(c + r, n_ctx), d), device_id_type=MESH)
    pl.semaphore_wait(barrier, n_db + n_ctx - 2)

    def columns(owner, k):
        return pl.ds(pl.multiple_of(owner * (width * chunks) + k * width, HDIM), width)

    here = pl.ds(d * group_size, group_size)
    z_copies, z_locals = [], []
    for k in range(chunks):
        row = []
        for r in range(1, n_db):
            peer = lax.rem(d + r, n_db)
            copy = pltpu.make_async_remote_copy(
                src_ref=kv.at[0, :, :, :, columns(peer, k)],
                dst_ref=stores[k].at[here],
                send_sem=z_send.at[k, r],
                recv_sem=z_recv.at[k, r],
                device_id=(c, peer),
                device_id_type=MESH,
            )
            copy.start()
            row.append(copy)
        z_copies.append(row)
        local = pltpu.make_async_copy(
            kv.at[0, :, :, :, columns(d, k)], stores[k].at[here], z_local.at[k]
        )
        local.start()
        z_locals.append(local)
    c_copies = []
    for k in range(chunks):
        z_locals[k].wait()
        for copy in z_copies[k]:
            copy.wait_recv()

        def place(i, carry, k=k):
            block = stores[k][ids[i]]
            to, slot = i // requests, lax.rem(i, requests)
            for h in range(heads):
                outgoing[k][to, h, slot] = block[:, :, h * HDIM : (h + 1) * HDIM]
            return carry

        lax.fori_loop(0, n_ctx * requests, place, 0)
        head_range = pl.ds(k * heads, heads)
        for r in range(1, n_ctx):
            peer = lax.rem(c + r, n_ctx)
            copy = pltpu.make_async_remote_copy(
                src_ref=outgoing[k].at[peer],
                dst_ref=out.at[head_range, :, c],
                send_sem=c_send.at[k, r],
                recv_sem=c_recv.at[k, r],
                device_id=(peer, d),
                device_id_type=MESH,
            )
            copy.start()
            c_copies.append(copy)
        local = pltpu.make_async_copy(
            outgoing[k].at[c], out.at[head_range, :, c], c_local.at[k]
        )
        local.start()
        z_locals.append(local)
    for row in z_copies:
        for copy in row:
            copy.wait_send()
    for local in z_locals[chunks:]:
        local.wait()
    for copy in c_copies:
        copy.wait()


def exchange(encoded_kv, neighbour_ids):
    n_ctx, n_db = lax.axis_size("ctx"), lax.axis_size("db")
    _, group_size, slab, two, full_width = encoded_kv.shape
    local_width = full_width // n_db
    heads = local_width // HDIM
    chunk_heads = 2 if heads % 2 == 0 else 1
    chunks = heads // chunk_heads
    stored = group_size * n_db
    requests = stored // n_ctx
    dtype = encoded_kv.dtype
    dma = pltpu.SemaphoreType.DMA
    return pl.pallas_call(
        functools.partial(exchange_kernel, n_ctx, n_db, chunks),
        out_shape=jax.ShapeDtypeStruct((heads, requests, n_ctx, slab, two, HDIM), dtype),
        in_specs=[
            pl.BlockSpec(memory_space=pltpu.SMEM),
            pl.BlockSpec(memory_space=pl.ANY),
        ],
        out_specs=pl.BlockSpec(memory_space=pl.ANY),
        scratch_shapes=[
            pltpu.VMEM((stored, slab, two, chunk_heads * HDIM), dtype) for _ in range(chunks)
        ]
        + [
            pltpu.VMEM((n_ctx, chunk_heads, requests, slab, two, HDIM), dtype)
            for _ in range(chunks)
        ]
        + [
            dma((chunks, n_db)),
            dma((chunks, n_db)),
            dma((chunks,)),
            dma((chunks, n_ctx)),
            dma((chunks, n_ctx)),
            dma((chunks,)),
        ],
        compiler_params=pltpu.CompilerParams(
            collective_id=0, has_side_effects=True, vmem_limit_bytes=32 * 1024 * 1024
        ),
        name="exchange",
    )(neighbour_ids, encoded_kv)


def attend_kernel(spans, q, kv, out):
    keys = kv.shape[1]
    odd = lax.rem(lax.broadcasted_iota(jnp.int32, (SPAN, keys), 1), 2) == 1
    for s in range(spans):
        rows = slice(s * SPAN, (s + 1) * SPAN)
        pairs = kv[s]
        scores = lax.dot_general(
            q[rows, :], pairs, (((1,), (1,)), ((), ())), preferred_element_type=jnp.float32
        ) * HDIM ** (-0.5)
        scores = jnp.where(odd, -jnp.inf, scores)
        exponent = jnp.exp(scores - jnp.max(scores, axis=-1, keepdims=True))
        weights = exponent / jnp.sum(exponent, axis=-1, keepdims=True)
        moved = pltpu.roll(weights, 1, 1).astype(jnp.bfloat16)
        mixed = jnp.dot(moved, pairs, preferred_element_type=jnp.float32)
        out[rows, :] = mixed.astype(jnp.bfloat16)


def attend(queries, pairs):
    rows, width = queries.shape
    heads, spans, keys, _ = pairs.shape
    return pl.pallas_call(
        functools.partial(attend_kernel, spans),
        grid=(heads,),
        out_shape=jax.ShapeDtypeStruct((rows, width), jnp.bfloat16),
        in_specs=[
            pl.BlockSpec((rows, HDIM), lambda h: (0, h)),
            pl.BlockSpec((None, spans, keys, HDIM), lambda h: (h, 0, 0, 0)),
        ],
        out_specs=pl.BlockSpec((rows, HDIM), lambda h: (0, h)),
        compiler_params=pltpu.CompilerParams(vmem_limit_bytes=32 * 1024 * 1024),
        name="attend",
    )(queries, pairs)


def on_device(stream, history, dwa_weights, w_query, w_out, encoded_kv, neighbour_ids):
    tok_rows = stream.shape[0]
    local_width = w_query.shape[1]
    spans_here = tok_rows // SPAN
    lead_rows = SPAN - 1
    full_stream = lax.all_gather(stream, "db", axis=1, tiled=True)
    queries = jnp.dot(
        full_stream,
        lax.all_gather(w_query, "ctx", axis=0, tiled=True),
        preferred_element_type=jnp.float32,
    ).astype(jnp.bfloat16)
    out_full = lax.all_gather(w_out, "ctx", axis=1, tiled=True)
    arrived = exchange(encoded_kv, neighbour_ids)
    pairs = arrived.reshape(local_width // HDIM, spans_here, -1, HDIM)
    following = shifted(queries[:lead_rows], "ctx", -1)
    grouped = jnp.concatenate([queries[lead_rows:], following], 0)
    mixed = attend(grouped, pairs)
    earlier = shifted(mixed[tok_rows - lead_rows :], "ctx", 1)
    attended = jnp.concatenate([earlier, mixed[: tok_rows - lead_rows]], 0)
    partial_value = jnp.dot(attended, out_full, preferred_element_type=jnp.float32)
    summed = lax.psum_scatter(
        partial_value.astype(jnp.bfloat16), "db", scatter_dimension=1, tiled=True
    ).astype(jnp.float32)
    block = stream.astype(jnp.float32) + summed
    dense = dwa_weights[-1] * block + jnp.sum(
        history.astype(jnp.float32) * dwa_weights[:-1, None, None], axis=0
    )
    return (block.astype(jnp.bfloat16), dense.astype(jnp.bfloat16))


def solution(mesh):
    placed = (
        P("ctx", "db"),
        P(None, "ctx", "db"),
        P(),
        P("ctx", "db"),
        P("db", "ctx"),
        P("db", None, "ctx", None, None),
        P(),
    )
    return jax.shard_map(
        on_device,
        mesh=mesh,
        in_specs=placed,
        out_specs=(P("ctx", "db"), P("ctx", "db")),
        check_vma=False,
    )
```

profile of v0, /device:TPU:0, one launch (start us, length us, event | category | flops | bytes accessed | tf_op | source)
XLA Modules:
  0.0 409.7 jit_solution(5103613057794724770)
XLA Ops:
  7.2 0.0 all-gather.4.cloned.1.call-start
  7.2 0.7 all-gather.4.cloned.1.call-update
  7.9 0.0 all-gather.6.cloned.1.call-start
  7.9 0.7 all-gather.6.cloned.1.call-update
  8.6 0.0 all-gather.8.cloned.1.call-start
  8.7 0.7 all-gather.8.cloned.1.call-update
  9.4 0.0 reduce-scatter.2.cloned.1.call-start
  9.4 66.3 %all-gather.4.cloned.1.call-done = bf16[384,4096]{1,0:T(8,128)(2,1)} async-done(((bf16[384,1024]{1,0:T(8,128)(2,1)}), bf16[384,4096]{1,0:T(8,128)(2,1)}) %all-gather.4.cloned.1.call-update) | async-done | bytes 3145744 | tf_op jit(solution)/shard_map/all_gather | solution.py:183
  75.8 55.0 %all-gather.6.cloned.1.call-done = bf16[4096,1024]{1,0:T(8,128)(2,1)} async-done(((bf16[512,1024]{1,0:T(8,128)(2,1)}), bf16[4096,1024]{1,0:T(8,128)(2,1)}) %all-gather.6.cloned.1.call-update) | async-done | bytes 8388624 | tf_op jit(solution)/shard_map/all_gather | solution.py:186
  130.8 7.7 %convolution_convert_fusion.1 = bf16[384,1024]{1,0:T(8,128)(2,1)S(1)} fusion(bf16[384,4096]{1,0:T(8,128)(2,1)} %all-gather.4.cloned.1.call-done, bf16[4096,1024]{1,0:T(8,128)(2,1)} %all-gather.6.cloned.1.call-done), kind=kOutput, calls=%fused_computation.5 | convolution fusion | flops 3221618688 | bytes 12320768 | tf_op jit(solution)/shard_map/dot_general | solution.py:184
  138.5 1.3 collective-permute-start
  139.9 3.2 copy-done
  143.0 153.7 %exchange.1 = bf16[8,12,8,16,2,128]{5,4,3,2,1,0:T(2,128)(2,1)S(1)} custom-call(s32[96]{0:T(128)S(1)} %copy-done.1, bf16[1,24,16,2,4096]{4,3,2,1,0:T(2,128)(2,1)S(1)} %copy-done), custom_call_target="tpu_custom_call" | custom-call | tf_op jit(solution)/shard_map/exchange/pallas_call | solution.py:114
  296.7 0.2 slice.24
  296.9 0.1 pad_maximum_fusion.q
  297.0 21.1 %attend.1 = bf16[384,1024]{1,0:T(8,128)(2,1)S(1)} custom-call(bf16[384,1024]{1,0:T(8,128)(2,1)S(1)} %pad_maximum_fusion.q, bf16[8,6,512,128]{3,2,1,0:T(8,128)(2,1)S(1)} %bitcast.6), custom_call_target="tpu_custom_call" | custom-call | tf_op jit(solution)/shard_map/attend/pallas_call | solution.py:164
  318.1 3.7 collective-permute-start.1
  322.0 0.9 collective-permute-done.1
  322.8 8.3 %convolution_convert_fusion = bf16[384,4096]{1,0:T(8,128)(2,1)} fusion(bf16[1024,4096]{1,0:T(8,128)(2,1)} %all-gather.8.cloned.1.call-done, bf16[321,1024]{1,0:T(8,128)(2,1)S(1)} %slice.27, bf16[63,1024]{1,0:T(8,128)(2,1)S(1)} %collective-permute-done.1), kind=kOutput, calls=%fused_computation.1 | convolution fusion | flops 3224371200 | bytes 12320768 | tf_op jit(solution)/shard_map/dot_general | solution.py:197
  331.1 0.6 copy-done.3
  331.7 0.6 slice.22
  332.3 4.7 %multiply_reduce_fusion = f32[384,1024]{1,0:T(8,128)S(1)} fusion(bf16[8,384,1024]{2,1,0:T(8,128)(2,1)} %param.8, f32[8]{0:T(128)S(1)} %bitcast.7), kind=kLoop, calls=%fused_computation | loop fusion | flops 9043968 | bytes 7864352 | tf_op jit(solution)/shard_map/reduce_sum | solution.py:202
  337.0 62.8 %reduce-scatter.2.cloned.1.call-done = bf16[384,1024]{1,0:T(8,128)(2,1)} async-done(((bf16[384,4096]{1,0:T(8,128)(2,1)}), bf16[384,1024]{1,0:T(8,128)(2,1)}) %reduce-scatter.2.cloned.1.call-update) | async-done | bytes 786448 | tf_op jit(solution)/shard_map/reduce_scatter | solution.py:198
  399.8 3.3 add_convert_fusion
  (12 shorter events, 0.1 us)
Async XLA Ops:
  7.2 68.6 %all-gather.4.cloned.1.call-start = ((), (), s32[]{:S(2)}) async-start(), calls=%async_computation.1 | async-start | bytes 3932160 | tf_op jit(solution)/shard_map/all_gather | solution.py:183
  7.9 122.9 %all-gather.6.cloned.1.call-start = ((), (), s32[]{:S(2)}) async-start(), calls=%async_computation.2 | async-start | bytes 9437184 | tf_op jit(solution)/shard_map/all_gather | solution.py:186
  8.6 313.3 %all-gather.8.cloned.1.call-start = ((), (), s32[]{:S(2)}) async-start(), calls=%async_computation.3 | async-start | bytes 9437184 | tf_op jit(solution)/shard_map/all_gather | solution.py:189
  9.4 130.4 %copy-start.1 = (s32[96]{0:T(128)S(1)}, s32[96]{0:T(128)}, u32[]{:S(2)}) copy-start(s32[96]{0:T(128)} %ids.1) | copy-start | bytes 1156
  9.4 390.4 %reduce-scatter.2.cloned.1.call-start = ((), (), s32[]{:S(2)}) async-start(), calls=%async_computation.4 | async-start | bytes 3932160 | tf_op jit(solution)/shard_map/reduce_scatter | solution.py:198
  138.5 158.3 %collective-permute-start = (bf16[63,1024]{1,0:T(8,128)(2,1)S(1)}, bf16[63,1024]{1,0:T(8,128)(2,1)S(1)}, u32[]{:S(2)}, u32[]{:S(2)}) collective-permute-start(bf16[63,1024]{1,0:T(8,128)(2,1)S(1)} %slice.25), channel_id=1, source_target_pairs={{4,0},{8,4},{12,8},{16,12},{20,16},{24,20},{28,24},{5,1},{9,5},{13... | collective-permute-start | bytes 387080 | tf_op jit(solution)/shard_map/ppermute | solution.py:19
  139.8 3.2 copy-start
  318.1 4.7 %collective-permute-start.1 = (bf16[63,1024]{1,0:T(8,128)(2,1)S(1)}, bf16[63,1024]{1,0:T(8,128)(2,1)S(1)}, u32[]{:S(2)}, u32[]{:S(2)}) collective-permute-start(bf16[63,1024]{1,0:T(8,128)(2,1)S(1)} %slice.26), channel_id=1, source_target_pairs={{0,4},{4,8},{8,12},{12,16},{16,20},{20,24},{24,28},{1,5},{5,9},{9,... | collective-permute-start | bytes 387080 | tf_op jit(solution)/shard_map/ppermute | solution.py:19
  331.1 0.7 copy-start.3
  332.3 67.5 %copy-start.2 = (bf16[384,1024]{1,0:T(8,128)(2,1)S(1)}, bf16[384,1024]{1,0:T(8,128)(2,1)}, u32[]{:S(2)}) copy-start(bf16[384,1024]{1,0:T(8,128)(2,1)} %param.7) | copy-start | bytes 2359300
Sparse Core Ops, SparseCore 0:
  9.6 66.1 all-gather.3
  77.6 53.0 all-gather.5
  132.6 70.6 all-gather.7
  331.2 68.5 reduce-scatter.1
where the time goes:
time: 410 us
  waiting for transfers between devices  187 us (46%)
  Pallas kernels  175 us (43%)
  matrix products  16 us (4%)
  between operations  13.9 us (3%)
  other arithmetic  8.1 us (2%)
  starting transfers between devices  5.18 us (1%)
  local copies, waits for them, and re-layouts  4.63 us (1%)
    pallas_call x1, Pallas kernels, exchange(): pl.pallas_call(functools.partial(exchange_kernel, n_ctx, n_db, chunks), o...  154 us
    all_gather x1, waiting for transfers between devices, on_device(): full_stream = lax.all_gather(stream, 'db', axis=1, tiled=True)  66.3 us
    reduce_scatter x1, waiting for transfers between devices, on_device(): lax.psum_scatter(partial_value.astype(jnp.bfloat16), 'db', scatter_dimens...  62.8 us
    all_gather x1, waiting for transfers between devices, on_device(): lax.all_gather(w_query, 'ctx', axis=0, tiled=True)  55 us
    pallas_call x1, Pallas kernels, attend(): pl.pallas_call(functools.partial(attend_kernel, spans), grid=(heads,), ou...  21.1 us
    dot_general x1, matrix products, on_device(): jnp.dot(attended, out_full, preferred_element_type=jnp.float32)  8.26 us
  transfers between devices with their start and end apart: 6, of which 4 were waited for; matrix products, arithmetic and copies ran while one was open for 3% of the time, Pallas kernels for 43%

commit v1 on v0

--- a/solution.py
+++ b/solution.py
@@ -19,9 +19,16 @@
     return lax.ppermute(block, axis, route)
 
 
-def exchange_kernel(n_ctx, n_db, chunks, ids, kv, out, *scratch):
+def partner(own, r, count):
+    if count & (count - 1):
+        return lax.rem(own + r, count)
+    bits = [1 << b for b in range(count.bit_length() - 1)]
+    return sum(lax.rem(own // bit + (1 if r & bit else 0), 2) * bit for bit in bits)
+
+
+def exchange_kernel(n_ctx, n_db, chunks, ids, kv, stream, out, full, *scratch):
     stores, outgoing = scratch[:chunks], scratch[chunks : 2 * chunks]
-    z_send, z_recv, z_local, c_send, c_recv, c_local = scratch[2 * chunks :]
+    z_send, z_recv, z_local, c_send, c_recv, c_local, s_send, s_recv, s_local = scratch[2 * chunks :]
     c, d = lax.axis_index("ctx"), lax.axis_index("db")
     group_size = kv.shape[1]
     width = stores[0].shape[3]
@@ -37,12 +44,58 @@
     def columns(owner, k):
         return pl.ds(pl.multiple_of(owner * (width * chunks) + k * width, HDIM), width)
 
+    own_width = stream.shape[1]
+
+    def block_of(owner):
+        return full.at[:, pl.ds(pl.multiple_of(owner * own_width, HDIM), own_width)]
+
+    def passing(step, side, owner):
+        return pltpu.make_async_remote_copy(
+            src_ref=stream if step == 0 else block_of(owner),
+            dst_ref=block_of(owner),
+            send_sem=s_send.at[(side + 1) // 2, step],
+            recv_sem=s_recv.at[(side + 1) // 2, step],
+            device_id=(c, d + side),
+            device_id_type=MESH,
+        )
+
+    def sends(step, side):
+        owner = d - side * step
+        return (owner >= 0) & (owner < n_db) & (d + side >= 0) & (d + side < n_db), owner
+
+    def pass_on(step):
+        for side in (-1, 1):
+            if step > 0:
+                take_in(step - 1, side)
+            live, owner = sends(step, side)
+
+            @pl.when(live)
+            def _(step=step, side=side, owner=owner):
+                passing(step, side, owner).start()
+
+    def take_in(step, side):
+        owner = d - side * (step + 1)
+
+        @pl.when((owner >= 0) & (owner < n_db))
+        def _():
+            pltpu.make_async_remote_copy(
+                src_ref=block_of(owner),
+                dst_ref=block_of(owner),
+                send_sem=s_send.at[(side + 1) // 2, step],
+                recv_sem=s_recv.at[(side + 1) // 2, step],
+                device_id=(c, d - side),
+                device_id_type=MESH,
+            ).wait_recv()
+
+    own = pltpu.make_async_copy(stream, block_of(d), s_local)
+    own.start()
+    pass_on(0)
     here = pl.ds(d * group_size, group_size)
     z_copies, z_locals = [], []
     for k in range(chunks):
         row = []
-        for r in range(1, n_db):
-            peer = lax.rem(d + r, n_db)
+        for r in reversed(range(1, n_db)):
+            peer = partner(d, r, n_db)
             copy = pltpu.make_async_remote_copy(
                 src_ref=kv.at[0, :, :, :, columns(peer, k)],
                 dst_ref=stores[k].at[here],
@@ -60,7 +113,10 @@
         local.start()
         z_locals.append(local)
     c_copies = []
+    steps = list(range(1, n_db - 1))
     for k in range(chunks):
+        if steps:
+            pass_on(steps.pop(0))
         z_locals[k].wait()
         for copy in z_copies[k]:
             copy.wait_recv()
@@ -91,6 +147,18 @@
         )
         local.start()
         z_locals.append(local)
+    for step in steps:
+        pass_on(step)
+    for side in (-1, 1):
+        take_in(n_db - 2, side)
+        for step in range(n_db - 1):
+            live, owner = sends(step, side)
+
+            @pl.when(live)
+            def _(step=step, side=side, owner=owner):
+                passing(step, side, owner).wait_send()
+
+    own.wait()
     for row in z_copies:
         for copy in row:
             copy.wait_send()
@@ -100,7 +168,7 @@
         copy.wait()
 
 
-def exchange(encoded_kv, neighbour_ids):
+def exchange(encoded_kv, neighbour_ids, stream):
     n_ctx, n_db = lax.axis_size("ctx"), lax.axis_size("db")
     _, group_size, slab, two, full_width = encoded_kv.shape
     local_width = full_width // n_db
@@ -113,12 +181,16 @@
     dma = pltpu.SemaphoreType.DMA
     return pl.pallas_call(
         functools.partial(exchange_kernel, n_ctx, n_db, chunks),
-        out_shape=jax.ShapeDtypeStruct((heads, requests, n_ctx, slab, two, HDIM), dtype),
+        out_shape=(
+            jax.ShapeDtypeStruct((heads, requests, n_ctx, slab, two, HDIM), dtype),
+            jax.ShapeDtypeStruct((stream.shape[0], full_width), stream.dtype),
+        ),
         in_specs=[
             pl.BlockSpec(memory_space=pltpu.SMEM),
+            pl.BlockSpec(memory_space=pltpu.HBM),
             pl.BlockSpec(memory_space=pl.ANY),
         ],
-        out_specs=pl.BlockSpec(memory_space=pl.ANY),
+        out_specs=(pl.BlockSpec(memory_space=pl.ANY), pl.BlockSpec(memory_space=pl.ANY)),
         scratch_shapes=[
             pltpu.VMEM((stored, slab, two, chunk_heads * HDIM), dtype) for _ in range(chunks)
         ]
@@ -133,29 +205,40 @@
             dma((chunks, n_ctx)),
             dma((chunks, n_ctx)),
             dma((chunks,)),
+            dma((2, n_db)),
+            dma((2, n_db)),
+            dma,
         ],
         compiler_params=pltpu.CompilerParams(
             collective_id=0, has_side_effects=True, vmem_limit_bytes=32 * 1024 * 1024
         ),
+        cost_estimate=pl.CostEstimate(
+            flops=0, bytes_accessed=96 * encoded_kv.size * encoded_kv.dtype.itemsize, transcendentals=0
+        ),
         name="exchange",
-    )(neighbour_ids, encoded_kv)
+    )(neighbour_ids, encoded_kv, stream)
 
 
 def attend_kernel(spans, q, kv, out):
     keys = kv.shape[1]
     odd = lax.rem(lax.broadcasted_iota(jnp.int32, (SPAN, keys), 1), 2) == 1
-    for s in range(spans):
-        rows = slice(s * SPAN, (s + 1) * SPAN)
-        pairs = kv[s]
-        scores = lax.dot_general(
-            q[rows, :], pairs, (((1,), (1,)), ((), ())), preferred_element_type=jnp.float32
-        ) * HDIM ** (-0.5)
-        scores = jnp.where(odd, -jnp.inf, scores)
-        exponent = jnp.exp(scores - jnp.max(scores, axis=-1, keepdims=True))
-        weights = exponent / jnp.sum(exponent, axis=-1, keepdims=True)
-        moved = pltpu.roll(weights, 1, 1).astype(jnp.bfloat16)
-        mixed = jnp.dot(moved, pairs, preferred_element_type=jnp.float32)
-        out[rows, :] = mixed.astype(jnp.bfloat16)
+    spread = [slice(s * SPAN, (s + 1) * SPAN) for s in range(spans)]
+    scores = [
+        lax.dot_general(
+            q[rows, :], kv[s], (((1,), (1,)), ((), ())), preferred_element_type=jnp.float32
+        )
+        for s, rows in enumerate(spread)
+    ]
+    scores = [jnp.where(odd, -jnp.inf, x * HDIM ** (-0.5)) for x in scores]
+    tops = [jnp.max(x, axis=-1, keepdims=True) for x in scores]
+    exponents = [jnp.exp(x - top) for x, top in zip(scores, tops)]
+    sums = [1.0 / jnp.sum(x, axis=-1, keepdims=True) for x in exponents]
+    weights = [pltpu.roll(x * total, 1, 1).astype(jnp.bfloat16) for x, total in zip(exponents, sums)]
+    mixed = [
+        jnp.dot(x, kv[s], preferred_element_type=jnp.float32) for s, x in enumerate(weights)
+    ]
+    for rows, x in zip(spread, mixed):
+        out[rows, :] = x.astype(jnp.bfloat16)
 
 
 def attend(queries, pairs):
@@ -180,14 +263,12 @@
     local_width = w_query.shape[1]
     spans_here = tok_rows // SPAN
     lead_rows = SPAN - 1
-    full_stream = lax.all_gather(stream, "db", axis=1, tiled=True)
-    queries = jnp.dot(
-        full_stream,
-        lax.all_gather(w_query, "ctx", axis=0, tiled=True),
-        preferred_element_type=jnp.float32,
-    ).astype(jnp.bfloat16)
+    query_full = lax.all_gather(w_query, "ctx", axis=0, tiled=True)
     out_full = lax.all_gather(w_out, "ctx", axis=1, tiled=True)
-    arrived = exchange(encoded_kv, neighbour_ids)
+    arrived, full_stream = exchange(encoded_kv, neighbour_ids, stream)
+    queries = jnp.dot(full_stream, query_full, preferred_element_type=jnp.float32).astype(
+        jnp.bfloat16
+    )
     pairs = arrived.reshape(local_width // HDIM, spans_here, -1, HDIM)
     following = shifted(queries[:lead_rows], "ctx", -1)
     grouped = jnp.concatenate([queries[lead_rows:], following], 0)

time: 410 us -> 351 us (0.86)
  waiting for transfers between devices: 187 us -> 95.9 us
  Pallas kernels: 175 us -> 204 us
    all_gather x2 -> x1, waiting for transfers between devices: 121 us -> 0.01 us  [on_device(): query_full = lax.all_gather(w_query, 'ctx', axis=0, tiled=True)]
    pallas_call x1, Pallas kernels: 154 us -> 196 us  [exchange(): pl.pallas_call(functools.partial(exchange_kernel, n_ctx, n_db, chunks), o...]
    reduce_scatter x1, waiting for transfers between devices: 62.8 us -> 91.8 us  [on_device(): lax.psum_scatter(partial_value.astype(jnp.bfloat16), 'db', scatter_dimens...]
    pallas_call x1, Pallas kernels: 21.1 us -> 8.12 us  [attend(): pl.pallas_call(functools.partial(attend_kernel, spans), grid=(heads,), ou...]
  transfers between devices with their start and end apart: 6 -> 5, of which waited for: 4 -> 3; matrix products, arithmetic and copies ran while one was open for 3% -> 3% of each run, Pallas kernels for 43% -> 58%
where the time goes in v1:
time: 351 us; the launch traced here: 350 us
  Pallas kernels  204 us (58%)
  waiting for transfers between devices  95.9 us (27%)
  matrix products  14.3 us (4%)
  between operations  13.9 us (4%)
  local copies, waits for them, and re-layouts  8.72 us (2%)
  other arithmetic  8.17 us (2%)
  starting transfers between devices  5.42 us (2%)
    pallas_call x1, Pallas kernels, exchange(): pl.pallas_call(functools.partial(exchange_kernel, n_ctx, n_db, chunks), o...  196 us
    reduce_scatter x1, waiting for transfers between devices, on_device(): lax.psum_scatter(partial_value.astype(jnp.bfloat16), 'db', scatter_dimens...  91.8 us
    dot_general x1, matrix products, on_device(): jnp.dot(attended, out_full, preferred_element_type=jnp.float32)  8.27 us
    pallas_call x1, Pallas kernels, attend(): pl.pallas_call(functools.partial(attend_kernel, spans), grid=(heads,), ou...  8.12 us
    unnamed x16, local copies, waits for them, and re-layouts  7.86 us
  transfers between devices with their start and end apart: 5, of which 3 were waited for; matrix products, arithmetic and copies ran while one was open for 3% of the time, Pallas kernels for 58%

profile of v1, /device:TPU:0, one launch (start us, length us, event | category | flops | bytes accessed | tf_op | source)
XLA Modules:
  0.0 350.4 jit_solution(13359532858206478593)
XLA Ops:
  7.2 0.0 all-gather.3.cloned.1.call-start
  7.2 0.7 all-gather.3.cloned.1.call-update
  7.9 0.0 all-gather.5.cloned.1.call-start
  7.9 0.7 all-gather.5.cloned.1.call-update
  8.6 0.0 reduce-scatter.2.cloned.1.call-start
  8.7 2.8 copy-done
  11.5 1.1 copy-done.2
  12.6 0.7 copy-done.4
  13.3 195.9 %exchange.1 = (bf16[8,12,8,16,2,128]{5,4,3,2,1,0:T(2,128)(2,1)S(1)}, bf16[384,4096]{1,0:T(8,128)(2,1)S(1)}) custom-call(s32[96]{0:T(128)S(1)} %copy-done.4, bf16[1,24,16,2,4096]{4,3,2,1,0:T(2,128)(2,1)S(1)} %copy-done, bf16[384,1024]{1,0:T(8,128)(2,1)S(1)} %copy-done.2), custom_call_target="tpu_custom_call" | custom-call | bytes 603979776 | tf_op jit(solution)/shard_map/exchange/pallas_call | solution.py:182
  209.2 2.7 copy-done.1
  211.9 6.0 %convolution_convert_fusion.1 = bf16[384,1024]{1,0:T(8,128)(2,1)S(1)} fusion(bf16[384,4096]{1,0:T(8,128)(2,1)S(1)} %get-tuple-element.4, bf16[4096,1024]{1,0:T(8,128)(2,1)} %all-gather.3.cloned.1.call-done), kind=kOutput, calls=%fused_computation.5 | convolution fusion | flops 3221618688 | bytes 12320768 | tf_op jit(solution)/shard_map/dot_general | solution.py:269
  217.9 1.3 collective-permute-start
  219.2 0.2 slice.24
  219.4 1.8 collective-permute-done
  221.2 0.1 pad_maximum_fusion.q
  221.3 8.1 %attend.1 = bf16[384,1024]{1,0:T(8,128)(2,1)S(1)} custom-call(bf16[384,1024]{1,0:T(8,128)(2,1)S(1)} %pad_maximum_fusion.q, bf16[8,6,512,128]{3,2,1,0:T(8,128)(2,1)S(1)} %bitcast.8), custom_call_target="tpu_custom_call" | custom-call | tf_op jit(solution)/shard_map/attend/pallas_call | solution.py:247
  229.5 4.0 %collective-permute-start.1 = (bf16[63,1024]{1,0:T(8,128)(2,1)S(1)}, bf16[63,1024]{1,0:T(8,128)(2,1)S(1)}, u32[]{:S(2)}, u32[]{:S(2)}) collective-permute-start(bf16[63,1024]{1,0:T(8,128)(2,1)S(1)} %slice.26), channel_id=1, source_target_pairs={{0,4},{4,8},{8,12},{12,16},{16,20},{20,24},{24,28},{1,5},{5,9},{9,... | collective-permute-start | bytes 387080 | tf_op jit(solution)/shard_map/ppermute | solution.py:19
  233.6 0.9 collective-permute-done.1
  234.4 8.3 %convolution_convert_fusion = bf16[384,4096]{1,0:T(8,128)(2,1)} fusion(bf16[1024,4096]{1,0:T(8,128)(2,1)} %all-gather.5.cloned.1.call-done, bf16[321,1024]{1,0:T(8,128)(2,1)S(1)} %slice.27, bf16[63,1024]{1,0:T(8,128)(2,1)S(1)} %collective-permute-done.1), kind=kOutput, calls=%fused_computation.1 | convolution fusion | flops 3224371200 | bytes 12320768 | tf_op jit(solution)/shard_map/dot_general | solution.py:278
  242.7 0.6 copy-done.5
  243.4 0.6 slice.22
  244.0 4.7 %multiply_reduce_fusion = f32[384,1024]{1,0:T(8,128)S(1)} fusion(bf16[8,384,1024]{2,1,0:T(8,128)(2,1)} %param.8, f32[8]{0:T(128)S(1)} %bitcast.9), kind=kLoop, calls=%fused_computation | loop fusion | flops 9043968 | bytes 7864352 | tf_op jit(solution)/shard_map/reduce_sum | solution.py:283
  248.7 91.8 %reduce-scatter.2.cloned.1.call-done = bf16[384,1024]{1,0:T(8,128)(2,1)} async-done(((bf16[384,4096]{1,0:T(8,128)(2,1)}), bf16[384,1024]{1,0:T(8,128)(2,1)}) %reduce-scatter.2.cloned.1.call-update) | async-done | bytes 786448 | tf_op jit(solution)/shard_map/reduce_scatter | solution.py:279
  340.5 3.4 add_convert_fusion
  (18 shorter events, 0.1 us)
Async XLA Ops:
  7.2 204.7 %all-gather.3.cloned.1.call-start = ((), (), s32[]{:S(2)}) async-start(), calls=%async_computation.1 | async-start | bytes 9437184 | tf_op jit(solution)/shard_map/all_gather | solution.py:266
  7.9 225.7 %all-gather.5.cloned.1.call-start = ((), (), s32[]{:S(2)}) async-start(), calls=%async_computation.2 | async-start | bytes 9437184 | tf_op jit(solution)/shard_map/all_gather | solution.py:267
  8.6 331.8 %reduce-scatter.2.cloned.1.call-start = ((), (), s32[]{:S(2)}) async-start(), calls=%async_computation.3 | async-start | bytes 3932160 | tf_op jit(solution)/shard_map/reduce_scatter | solution.py:279
  8.7 2.8 copy-start
  11.5 1.1 copy-start.2
  12.6 0.7 copy-start.4
  209.2 2.7 copy-start.1
  211.9 9.4 %slice-start = ((s8[6291456]{0:T(1024)(128)(4,1)}), s8[4194304]{0:T(1024)(128)(4,1)S(1)}, s32[]{:S(2)}) async-start(s8[6291456]{0:T(1024)(128)(4,1)} %bitcast.6), calls=%async_computation.4 | async-start | bytes 8388608
  211.9 9.4 %slice-start.1 = ((s8[6291456]{0:T(1024)(128)(4,1)}), s8[2097152]{0:T(1024)(128)(4,1)S(1)}, s32[]{:S(2)}) async-start(s8[6291456]{0:T(1024)(128)(4,1)} %bitcast.6), calls=%async_computation.5 | async-start | bytes 4194304
  217.9 3.2 collective-permute-start
  229.5 5.0 %collective-permute-start.1 = (bf16[63,1024]{1,0:T(8,128)(2,1)S(1)}, bf16[63,1024]{1,0:T(8,128)(2,1)S(1)}, u32[]{:S(2)}, u32[]{:S(2)}) collective-permute-start(bf16[63,1024]{1,0:T(8,128)(2,1)S(1)} %slice.26), channel_id=1, source_target_pairs={{0,4},{4,8},{8,12},{12,16},{16,20},{20,24},{24,28},{1,5},{5,9},{9,... | collective-permute-start | bytes 387080 | tf_op jit(solution)/shard_map/ppermute | solution.py:19
  242.7 0.7 copy-start.5
  244.0 96.5 %copy-start.3 = (bf16[384,1024]{1,0:T(8,128)(2,1)S(1)}, bf16[384,1024]{1,0:T(8,128)(2,1)}, u32[]{:S(2)}) copy-start(bf16[384,1024]{1,0:T(8,128)(2,1)} %stream.1) | copy-start | bytes 2359300
Sparse Core Ops, SparseCore 0:
  9.9 57.0 all-gather.2
  68.9 67.5 all-gather.4
  242.9 97.5 reduce-scatter.1
